TPU v7x, 128 devices: a whole 4x4x4 slice. The times are simulated.
128 devices in a mesh: inst: 8 (over z_hi, x), slab: 16 (over z_lo, y, core).
Axes of the slice: x: 4, y: 4, z: 4 (z_hi: 2, z_lo: 2; z = z_hi * 2 + z_lo), core: 2. Of those that a mesh axis runs over, the one named last changes fastest.
Arguments:
- prior_disp: float32 [16, 3, 32, 128, 512], P('inst', None, 'slab'), may hold values from -6 to 6
- surface_disp: float32 [16, 3, 16384], P('inst', None, 'slab'), may hold values from -6 to 6
- springs: float32 [3, 32, 128, 512], P(None, 'slab'), may hold values from 0.2 to 5
- wall_row: int32 [32, 512], P('slab'), may hold values from 0 to 16383
- wall_mask: int32 [32, 512], P('slab'), may hold values 0 or 1
Outputs:
- displacement: float32 [16, 3, 32, 128, 512], P('inst', None, 'slab')
- grid_velocity: float32 [16, 3, 32, 128, 512], P('inst', None, 'slab')
Inputs may be any that keep to these rules, and one draw needn't show every extreme that they name: `wall_row`: each wall cell names one structural surface node.
All inputs are finite; a program needn't handle non-finite values. No bound on the sum of `wall_mask` on one device may be relied on, other than what follows from the above.
Results may differ from a plain program's by a relative error of at most 0.000078.
Values sent between devices are 32-bit elements; how exact they have to be, the bound alone decides.
A program may use at most 128 MiB of HBM per device.

v0:
```python
import jax
import jax.numpy as jnp
from jax import lax
from jax.sharding import PartitionSpec as P

SWEEPS = 8


RELAXATION = 0.9


def padded_2(block, sides, width):
    for axis, dim in sides:
        count = lax.axis_size(axis)
        forward = [(i, i + 1) for i in range(count - 1)]
        backward = [(target, source) for source, target in forward]
        low = lax.ppermute(
            lax.slice_in_dim(block, block.shape[dim] - width, None, axis=dim), axis, forward
        )
        high = lax.ppermute(lax.slice_in_dim(block, 0, width, axis=dim), axis, backward)
        block = jnp.concatenate([low, block, high], axis=dim)
    return block


def relax_sweep(padded, springs, wall_disp, released):
    centre = padded[:, :, 1:-1]
    along_planes = padded[:, :, 2:] + padded[:, :, :-2]
    ghost_row = wall_disp + released * centre[:, :, :, 0, :]
    row_below = jnp.concatenate([ghost_row[:, :, :, None, :], centre[:, :, :, :-1, :]], axis=3)
    row_above = jnp.concatenate(
        [centre[:, :, :, 1:, :], jnp.zeros_like(centre[:, :, :, :1, :])], axis=3
    )
    beside_all = jnp.roll(centre, 1, axis=4) + jnp.roll(centre, -1, axis=4)
    weighted = (
        springs[0] * along_planes + springs[1] * (row_below + row_above) + springs[2] * beside_all
    )
    weight = 2.0 * (springs[0] + springs[1] + springs[2])
    return centre + RELAXATION * (weighted / weight - centre)


def spectral(row_inst, col_inst, total_inst):
    offset = row_inst[:, None] - col_inst[None, :]
    parity = 1.0 - 2.0 * jnp.mod(offset, 2).astype(jnp.float32)
    phase_angle = jnp.pi * offset.astype(jnp.float32) / total_inst
    guarded = jnp.where(offset == 0, jnp.float32(0.5 * jnp.pi), phase_angle)
    entries = 0.5 * parity * jnp.cos(guarded) / jnp.sin(guarded)
    entries = jnp.where(offset == 0, jnp.float32(0.0), entries)
    return 2.0 * jnp.pi / total_inst * entries


def per_device(prior_disp, surface_disp, springs, wall_row, wall_mask):
    inst_here = prior_disp.shape[0]
    full_surface = lax.all_gather(surface_disp, "slab", axis=2, tiled=True)
    picked = jnp.take(full_surface, wall_row, axis=2)
    clamped = wall_mask.astype(jnp.float32)
    released = 1.0 - clamped
    wall_disp = clamped * picked
    displaced = prior_disp
    for sweep_index in range(SWEEPS):
        padded = padded_2(displaced, (("slab", 2),), 1)
        displaced = relax_sweep(padded, springs, wall_disp, released)
    total_inst = inst_here * lax.axis_size("inst")
    everyone = jnp.arange(total_inst, dtype=jnp.int32)
    matrix = spectral(everyone, everyone, total_inst)
    time_rate = jnp.einsum(
        "ik,kcpjl->icpjl",
        matrix,
        lax.all_to_all(displaced, "inst", split_axis=3, concat_axis=0, tiled=True),
        precision=lax.Precision.HIGHEST,
    )
    grid_velocity = lax.all_to_all(time_rate, "inst", split_axis=0, concat_axis=3, tiled=True)
    return (displaced, grid_velocity)


def solution(mesh):
    in_specs = (
        P("inst", None, "slab", None, None),
        P("inst", None, "slab"),
        P(None, "slab", None, None),
        P("slab", None),
        P("slab", None),
    )
    out_specs = (P("inst", None, "slab", None, None), P("inst", None, "slab", None, None))
    return jax.shard_map(
        per_device, mesh=mesh, in_specs=in_specs, out_specs=out_specs, check_vma=False
    )
```

profile of v0, /device:TPU:32, one launch (start us, length us, event | category | flops | bytes accessed | tf_op | source)
XLA Modules:
  0.0 543.6 jit_solution(4009025699690766264)
XLA Ops:
  16.7 30.0 %all_gather.3 = f32[2,3,16384]{2,0,1:T(2,128)S(1)} all-gather(f32[2,3,1024]{2,0,1:T(2,128)S(1)} %copy-done.13), channel_id=1, replica_groups=mesh['inst'=8,'slab'=16] {'slab'}, dimensions={2}, use_global_device_ids=true | all-gather | bytes 417792 | tf_op jit(solution)/shard_map/all_gather | solution.py:53
  49.1 15.1 %copy.39 = f32[2,3,16384]{1,0,2:T(2,128)} copy(f32[2,3,16384]{2,0,1:T(2,128)S(1)} %all_gather.3) | data formatting | bytes 786432 | tf_op jit(solution)/shard_map/all_gather | solution.py:53
  64.2 13.3 %gather_fusion = f32[1024,2,3]{2,1,0:T(2,128)} fusion(f32[2,3,16384]{1,0,2:T(2,128)} %copy.39, s32[1024]{0:T(1024)S(1)} %broadcast_clamp_fusion), kind=kCustom, calls=%fused_computation | custom fusion | bytes 53248 | tf_op jit(solution)/shard_map/jit(_take)/gather | solution.py:54
  93.8 17.1 %multiply_add_fusion.7 = f32[2,3,2,128,512]{4,2,1,0,3:T(2,128)S(1)} fusion(f32[2,3,2,128,512]{4,2,1,0,3:T(2,128)S(1)} %copy.52, f32[2,3,2,128,1]{4,2,1,0,3:T(2,128)} %get-tuple-element.67, f32[2,3,2,128,511]{4,2,1,0,3:T(2,128)S(1)} %get-tuple-element.69, f32[2,3,2,128,511]{4,2,1,0,3:T(2,128)S(1)} %get-tuple-element.68, ...), kind=kLoop, calls=%fused_computation.97 | loop fusion | flops 13369344 | bytes 24092672 | tf_op jit(solution)/shard_map/add | solution.py:38
  127.0 7.8 %collective-permute-done.2 = f32[2,3,1,128,512]{4,2,1,0,3:T(1,128)} collective-permute-done((f32[2,3,1,128,512]{4,2,1,0,3:T(1,128)}, f32[2,3,1,128,512]{4,2,1,0,3:T(1,128)}, u32[]{:S(2)}, u32[]{:S(2)}) %collective-permute-start.2) | collective-permute-done | bytes 1572896 | tf_op jit(solution)/shard_map/ppermute | solution.py:20
  134.7 5.6 %collective-permute-done.3 = f32[2,3,1,128,512]{4,2,1,0,3:T(1,128)S(1)} collective-permute-done((f32[2,3,1,128,512]{4,2,1,0,3:T(1,128)S(1)}, f32[2,3,1,128,512]{4,2,1,0,3:T(1,128)S(1)}, u32[]{:S(2)}, u32[]{:S(2)}) %collective-permute-start.3) | collective-permute-done | bytes 1572896 | tf_op jit(solution)/shard_map/ppermute | solution.py:17
  141.5 16.6 %multiply_add_fusion.6 = f32[2,3,2,128,512]{4,2,1,0,3:T(2,128)S(1)} fusion(f32[2,3,2,128,512]{4,2,1,0,3:T(2,128)S(1)} %multiply_add_fusion.7, f32[2,3,2,128,1]{4,2,1,0,3:T(2,128)} %get-tuple-element.59, f32[2,3,2,128,511]{4,2,1,0,3:T(2,128)S(1)} %get-tuple-element.61, f32[2,3,2,128,511]{4,2,1,0,3:T(2,128)S(1)} %get-tuple-element.60, ...), kind=kLoop, calls=%fused_computation.96 | loop fusion | flops 13369344 | bytes 24092672 | tf_op jit(solution)/shard_map/add | solution.py:38
  174.3 7.5 %collective-permute-done.4 = f32[2,3,1,128,512]{4,2,1,0,3:T(1,128)} collective-permute-done((f32[2,3,1,128,512]{4,2,1,0,3:T(1,128)}, f32[2,3,1,128,512]{4,2,1,0,3:T(1,128)}, u32[]{:S(2)}, u32[]{:S(2)}) %collective-permute-start.4) | collective-permute-done | bytes 1572896 | tf_op jit(solution)/shard_map/ppermute | solution.py:20
  181.8 5.6 %collective-permute-done.5 = f32[2,3,1,128,512]{4,2,1,0,3:T(1,128)S(1)} collective-permute-done((f32[2,3,1,128,512]{4,2,1,0,3:T(1,128)S(1)}, f32[2,3,1,128,512]{4,2,1,0,3:T(1,128)S(1)}, u32[]{:S(2)}, u32[]{:S(2)}) %collective-permute-start.5) | collective-permute-done | bytes 1572896 | tf_op jit(solution)/shard_map/ppermute | solution.py:17
  188.5 16.6 %multiply_add_fusion.5 = f32[2,3,2,128,512]{4,2,1,0,3:T(2,128)S(1)} fusion(f32[2,3,2,128,512]{4,2,1,0,3:T(2,128)S(1)} %multiply_add_fusion.6, f32[2,3,2,128,1]{4,2,1,0,3:T(2,128)} %get-tuple-element.51, f32[2,3,2,128,511]{4,2,1,0,3:T(2,128)S(1)} %get-tuple-element.53, f32[2,3,2,128,511]{4,2,1,0,3:T(2,128)S(1)} %get-tuple-element.52, ...), kind=kLoop, calls=%fused_computation.95 | loop fusion | flops 13369344 | bytes 24092672 | tf_op jit(solution)/shard_map/add | solution.py:38
  221.6 7.3 %collective-permute-done.6 = f32[2,3,1,128,512]{4,2,1,0,3:T(1,128)} collective-permute-done((f32[2,3,1,128,512]{4,2,1,0,3:T(1,128)}, f32[2,3,1,128,512]{4,2,1,0,3:T(1,128)}, u32[]{:S(2)}, u32[]{:S(2)}) %collective-permute-start.6) | collective-permute-done | bytes 1572896 | tf_op jit(solution)/shard_map/ppermute | solution.py:20
  235.6 16.6 %multiply_add_fusion.4 = f32[2,3,2,128,512]{4,2,1,0,3:T(2,128)S(1)} fusion(f32[2,3,2,128,512]{4,2,1,0,3:T(2,128)S(1)} %multiply_add_fusion.5, f32[2,3,2,128,1]{4,2,1,0,3:T(2,128)} %get-tuple-element.43, f32[2,3,2,128,511]{4,2,1,0,3:T(2,128)S(1)} %get-tuple-element.45, f32[2,3,2,128,511]{4,2,1,0,3:T(2,128)S(1)} %get-tuple-element.44, ...), kind=kLoop, calls=%fused_computation.94 | loop fusion | flops 13369344 | bytes 24092672 | tf_op jit(solution)/shard_map/add | solution.py:38
  268.4 7.5 %collective-permute-done.8 = f32[2,3,1,128,512]{4,2,1,0,3:T(1,128)} collective-permute-done((f32[2,3,1,128,512]{4,2,1,0,3:T(1,128)}, f32[2,3,1,128,512]{4,2,1,0,3:T(1,128)}, u32[]{:S(2)}, u32[]{:S(2)}) %collective-permute-start.8) | collective-permute-done | bytes 1572896 | tf_op jit(solution)/shard_map/ppermute | solution.py:20
  282.6 16.6 %multiply_add_fusion.3 = f32[2,3,2,128,512]{4,2,1,0,3:T(2,128)S(1)} fusion(f32[2,3,2,128,512]{4,2,1,0,3:T(2,128)S(1)} %multiply_add_fusion.4, f32[2,3,2,128,1]{4,2,1,0,3:T(2,128)} %get-tuple-element.35, f32[2,3,2,128,511]{4,2,1,0,3:T(2,128)S(1)} %get-tuple-element.37, f32[2,3,2,128,511]{4,2,1,0,3:T(2,128)S(1)} %get-tuple-element.36, ...), kind=kLoop, calls=%fused_computation.93 | loop fusion | flops 13369344 | bytes 24092672 | tf_op jit(solution)/shard_map/add | solution.py:38
  315.7 7.3 %collective-permute-done.10 = f32[2,3,1,128,512]{4,2,1,0,3:T(1,128)} collective-permute-done((f32[2,3,1,128,512]{4,2,1,0,3:T(1,128)}, f32[2,3,1,128,512]{4,2,1,0,3:T(1,128)}, u32[]{:S(2)}, u32[]{:S(2)}) %collective-permute-start.10) | collective-permute-done | bytes 1572896 | tf_op jit(solution)/shard_map/ppermute | solution.py:20
  322.9 5.6 %collective-permute-done.11 = f32[2,3,1,128,512]{4,2,1,0,3:T(1,128)S(1)} collective-permute-done((f32[2,3,1,128,512]{4,2,1,0,3:T(1,128)S(1)}, f32[2,3,1,128,512]{4,2,1,0,3:T(1,128)S(1)}, u32[]{:S(2)}, u32[]{:S(2)}) %collective-permute-start.11) | collective-permute-done | bytes 1572896 | tf_op jit(solution)/shard_map/ppermute | solution.py:17
  329.7 16.6 %multiply_add_fusion.2 = f32[2,3,2,128,512]{4,2,1,0,3:T(2,128)S(1)} fusion(f32[2,3,2,128,512]{4,2,1,0,3:T(2,128)S(1)} %multiply_add_fusion.3, f32[2,3,2,128,1]{4,2,1,0,3:T(2,128)} %get-tuple-element.27, f32[2,3,2,128,511]{4,2,1,0,3:T(2,128)S(1)} %get-tuple-element.29, f32[2,3,2,128,511]{4,2,1,0,3:T(2,128)S(1)} %get-tuple-element.28, ...), kind=kLoop, calls=%fused_computation.92 | loop fusion | flops 13369344 | bytes 24092672 | tf_op jit(solution)/shard_map/add | solution.py:38
  362.5 7.5 %collective-permute-done.12 = f32[2,3,1,128,512]{4,2,1,0,3:T(1,128)} collective-permute-done((f32[2,3,1,128,512]{4,2,1,0,3:T(1,128)}, f32[2,3,1,128,512]{4,2,1,0,3:T(1,128)}, u32[]{:S(2)}, u32[]{:S(2)}) %collective-permute-start.12) | collective-permute-done | bytes 1572896 | tf_op jit(solution)/shard_map/ppermute | solution.py:20
  376.7 16.6 %multiply_add_fusion.1 = f32[2,3,2,128,512]{4,2,1,0,3:T(2,128)S(1)} fusion(f32[2,3,2,128,512]{4,2,1,0,3:T(2,128)S(1)} %multiply_add_fusion.2, f32[2,3,2,128,1]{4,2,1,0,3:T(2,128)} %get-tuple-element.19, f32[2,3,2,128,511]{4,2,1,0,3:T(2,128)S(1)} %get-tuple-element.21, f32[2,3,2,128,511]{4,2,1,0,3:T(2,128)S(1)} %get-tuple-element.20, ...), kind=kLoop, calls=%fused_computation.91 | loop fusion | flops 13369344 | bytes 24092672 | tf_op jit(solution)/shard_map/add | solution.py:38
  410.2 6.8 %collective-permute-done.14 = f32[2,3,1,128,512]{4,2,1,0,3:T(1,128)} collective-permute-done((f32[2,3,1,128,512]{4,2,1,0,3:T(1,128)}, f32[2,3,1,128,512]{4,2,1,0,3:T(1,128)}, u32[]{:S(2)}, u32[]{:S(2)}) %collective-permute-start.14) | collective-permute-done | bytes 1572896 | tf_op jit(solution)/shard_map/ppermute | solution.py:20
  417.0 5.6 %collective-permute-done.15 = f32[2,3,1,128,512]{4,2,1,0,3:T(1,128)S(1)} collective-permute-done((f32[2,3,1,128,512]{4,2,1,0,3:T(1,128)S(1)}, f32[2,3,1,128,512]{4,2,1,0,3:T(1,128)S(1)}, u32[]{:S(2)}, u32[]{:S(2)}) %collective-permute-start.15) | collective-permute-done | bytes 1572896 | tf_op jit(solution)/shard_map/ppermute | solution.py:17
  423.8 16.5 %multiply_add_fusion = f32[2,3,2,128,512]{4,2,1,0,3:T(2,128)S(1)} fusion(f32[2,3,2,128,512]{4,2,1,0,3:T(2,128)S(1)} %multiply_add_fusion.1, f32[2,3,2,128,1]{4,2,1,0,3:T(2,128)S(1)} %get-tuple-element.11, f32[2,3,2,128,511]{4,2,1,0,3:T(2,128)S(1)} %get-tuple-element.13, f32[2,3,2,128,511]{4,2,1,0,3:T(2,128)S(1)} %get-tuple-element.12, ...), kind=kLoop, calls=%fused_computation.90 | loop fusion | flops 13369344 | bytes 24092672 | tf_op jit(solution)/shard_map/add | solution.py:38
  440.3 42.8 %all_to_all.36 = f32[2,3,2,128,512]{4,2,1,0,3:T(2,128)S(1)} all-to-all(f32[2,3,2,128,512]{4,2,1,0,3:T(2,128)S(1)} %multiply_add_fusion), channel_id=1, replica_groups=mesh['inst'=8,'slab'=16] {'inst'}, dimensions={3} | all-to-all | bytes 6291456 | tf_op jit(solution)/shard_map/all_to_all | solution.py:68
  507.3 31.7 %all-to-all-done.1 = f32[16,3,2,16,512]{4,3,2,1,0:T(8,128)} async-done(((f32[16,3,2,16,512]{4,3,2,1,0:T(8,128)}), f32[16,3,2,16,512]{4,3,2,1,0:T(8,128)}, u32[]{:S(2)}, u32[]{:S(2)}) %all-to-all-start.1) | async-done | bytes 3145760 | tf_op jit(solution)/shard_map/all_to_all | solution.py:71
  (116 shorter events, 202.0 us)
Async XLA Ops:
  2.8 11.6 %copy-start.14 = (s32[2,512]{1,0:T(2,128)S(1)}, s32[2,512]{1,0:T(2,128)}, u32[]{:S(2)}) copy-start(s32[2,512]{1,0:T(2,128)} %param.8) | copy-start | bytes 12292
  2.8 11.7 %copy-start.4 = (f32[3,2,128,512]{3,2,1,0:T(8,128)S(1)}, f32[3,2,128,512]{3,2,1,0:T(8,128)}, u32[]{:S(2)}) copy-start(f32[3,2,128,512]{3,2,1,0:T(8,128)} %param.7) | copy-start | bytes 4718596
  5.6 88.2 %collective-permute-start = (f32[2,3,1,128,512]{4,2,1,0,3:T(1,128)}, f32[2,3,1,128,512]{4,2,1,0,3:T(1,128)}, u32[]{:S(2)}, u32[]{:S(2)}) collective-permute-start(f32[2,3,1,128,512]{4,2,1,0,3:T(1,128)} %copy.34), channel_id=1, source_target_pairs={{1,0},{2,1},{3,2},{4,3},{5,4},{6,5},{7,6},{8,7},{9,8},{10,9},{11,1... | collective-permute-start | bytes 4718600 | tf_op jit(solution)/shard_map/ppermute | solution.py:20
  12.3 34.4 %copy-start.3 = (f32[2,3,2,128,512]{4,3,2,1,0:T(8,128)S(1)}, f32[2,3,2,128,512]{4,3,2,1,0:T(8,128)}, u32[]{:S(2)}) copy-start(f32[2,3,2,128,512]{4,3,2,1,0:T(8,128)} %param.5) | copy-start | bytes 9437188
  12.3 81.5 %collective-permute-start.1 = (f32[2,3,1,128,512]{4,2,1,0,3:T(1,128)}, f32[2,3,1,128,512]{4,2,1,0,3:T(1,128)}, u32[]{:S(2)}, u32[]{:S(2)}) collective-permute-start(f32[2,3,1,128,512]{4,2,1,0,3:T(1,128)} %copy.36), channel_id=1, source_target_pairs={{0,1},{1,2},{2,3},{3,4},{4,5},{5,6},{6,7},{7,8},{8,9},{9,10},{10,1... | collective-permute-start | bytes 4718600 | tf_op jit(solution)/shard_map/ppermute | solution.py:17
  78.9 4.8 copy-start.5
  80.5 13.3 %copy-start = (f32[2,128,512]{2,0,1:T(2,128)}, f32[2,128,512]{2,0,1:T(2,128)S(1)}, u32[]{:S(2)}) copy-start(f32[2,128,512]{2,0,1:T(2,128)S(1)} %copy.33) | copy-start | bytes 1572868
  82.1 11.7 %copy-start.1 = (f32[2,128,512]{2,0,1:T(2,128)}, f32[2,128,512]{2,0,1:T(2,128)S(1)}, u32[]{:S(2)}) copy-start(f32[2,128,512]{2,0,1:T(2,128)S(1)} %copy.38) | copy-start | bytes 1572868
  83.8 10.1 %copy-start.2 = (f32[2,128,512]{2,0,1:T(2,128)}, f32[2,128,512]{2,0,1:T(2,128)S(1)}, u32[]{:S(2)}) copy-start(f32[2,128,512]{2,0,1:T(2,128)S(1)} %copy.45) | copy-start | bytes 1572868
  114.5 20.2 %collective-permute-start.2 = (f32[2,3,1,128,512]{4,2,1,0,3:T(1,128)}, f32[2,3,1,128,512]{4,2,1,0,3:T(1,128)}, u32[]{:S(2)}, u32[]{:S(2)}) collective-permute-start(f32[2,3,1,128,512]{4,2,1,0,3:T(1,128)} %get-tuple-element.54), channel_id=1, source_target_pairs={{1,0},{2,1},{3,2},{4,3},{5,4},{6,5},{7,6},{8,7},{9,8},{10,9},{11,1... | collective-permute-start | bytes 4718600 | tf_op jit(solution)/shard_map/ppermute | solution.py:20
  116.5 23.8 %collective-permute-start.3 = (f32[2,3,1,128,512]{4,2,1,0,3:T(1,128)S(1)}, f32[2,3,1,128,512]{4,2,1,0,3:T(1,128)S(1)}, u32[]{:S(2)}, u32[]{:S(2)}) collective-permute-start(f32[2,3,1,128,512]{4,2,1,0,3:T(1,128)S(1)} %get-tuple-element.55), channel_id=1, source_target_pairs={{0,1},{1,2},{2,3},{3,4},{4,5},{5,6},{6,7},{7,8},{8,9},{9,10},{10,1... | collective-permute-start | bytes 4718600 | tf_op jit(solution)/shard_map/ppermute | solution.py:17
  161.6 20.1 %collective-permute-start.4 = (f32[2,3,1,128,512]{4,2,1,0,3:T(1,128)}, f32[2,3,1,128,512]{4,2,1,0,3:T(1,128)}, u32[]{:S(2)}, u32[]{:S(2)}) collective-permute-start(f32[2,3,1,128,512]{4,2,1,0,3:T(1,128)} %get-tuple-element.46), channel_id=1, source_target_pairs={{1,0},{2,1},{3,2},{4,3},{5,4},{6,5},{7,6},{8,7},{9,8},{10,9},{11,1... | collective-permute-start | bytes 4718600 | tf_op jit(solution)/shard_map/ppermute | solution.py:20
  163.5 23.8 %collective-permute-start.5 = (f32[2,3,1,128,512]{4,2,1,0,3:T(1,128)S(1)}, f32[2,3,1,128,512]{4,2,1,0,3:T(1,128)S(1)}, u32[]{:S(2)}, u32[]{:S(2)}) collective-permute-start(f32[2,3,1,128,512]{4,2,1,0,3:T(1,128)S(1)} %get-tuple-element.47), channel_id=1, source_target_pairs={{0,1},{1,2},{2,3},{3,4},{4,5},{5,6},{6,7},{7,8},{8,9},{9,10},{10,1... | collective-permute-start | bytes 4718600 | tf_op jit(solution)/shard_map/ppermute | solution.py:17
  208.7 20.1 %collective-permute-start.6 = (f32[2,3,1,128,512]{4,2,1,0,3:T(1,128)}, f32[2,3,1,128,512]{4,2,1,0,3:T(1,128)}, u32[]{:S(2)}, u32[]{:S(2)}) collective-permute-start(f32[2,3,1,128,512]{4,2,1,0,3:T(1,128)} %get-tuple-element.38), channel_id=1, source_target_pairs={{1,0},{2,1},{3,2},{4,3},{5,4},{6,5},{7,6},{8,7},{9,8},{10,9},{11,1... | collective-permute-start | bytes 4718600 | tf_op jit(solution)/shard_map/ppermute | solution.py:20
  210.6 23.8 %collective-permute-start.7 = (f32[2,3,1,128,512]{4,2,1,0,3:T(1,128)S(1)}, f32[2,3,1,128,512]{4,2,1,0,3:T(1,128)S(1)}, u32[]{:S(2)}, u32[]{:S(2)}) collective-permute-start(f32[2,3,1,128,512]{4,2,1,0,3:T(1,128)S(1)} %get-tuple-element.39), channel_id=1, source_target_pairs={{0,1},{1,2},{2,3},{3,4},{4,5},{5,6},{6,7},{7,8},{8,9},{9,10},{10,1... | collective-permute-start | bytes 4718600 | tf_op jit(solution)/shard_map/ppermute | solution.py:17
  255.7 20.1 %collective-permute-start.8 = (f32[2,3,1,128,512]{4,2,1,0,3:T(1,128)}, f32[2,3,1,128,512]{4,2,1,0,3:T(1,128)}, u32[]{:S(2)}, u32[]{:S(2)}) collective-permute-start(f32[2,3,1,128,512]{4,2,1,0,3:T(1,128)} %get-tuple-element.30), channel_id=1, source_target_pairs={{1,0},{2,1},{3,2},{4,3},{5,4},{6,5},{7,6},{8,7},{9,8},{10,9},{11,1... | collective-permute-start | bytes 4718600 | tf_op jit(solution)/shard_map/ppermute | solution.py:20
  257.6 23.8 %collective-permute-start.9 = (f32[2,3,1,128,512]{4,2,1,0,3:T(1,128)S(1)}, f32[2,3,1,128,512]{4,2,1,0,3:T(1,128)S(1)}, u32[]{:S(2)}, u32[]{:S(2)}) collective-permute-start(f32[2,3,1,128,512]{4,2,1,0,3:T(1,128)S(1)} %get-tuple-element.31), channel_id=1, source_target_pairs={{0,1},{1,2},{2,3},{3,4},{4,5},{5,6},{6,7},{7,8},{8,9},{9,10},{10,1... | collective-permute-start | bytes 4718600 | tf_op jit(solution)/shard_map/ppermute | solution.py:17
  302.8 20.1 %collective-permute-start.10 = (f32[2,3,1,128,512]{4,2,1,0,3:T(1,128)}, f32[2,3,1,128,512]{4,2,1,0,3:T(1,128)}, u32[]{:S(2)}, u32[]{:S(2)}) collective-permute-start(f32[2,3,1,128,512]{4,2,1,0,3:T(1,128)} %get-tuple-element.22), channel_id=1, source_target_pairs={{1,0},{2,1},{3,2},{4,3},{5,4},{6,5},{7,6},{8,7},{9,8},{10,9},{11,1... | collective-permute-start | bytes 4718600 | tf_op jit(solution)/shard_map/ppermute | solution.py:20
  304.7 23.8 %collective-permute-start.11 = (f32[2,3,1,128,512]{4,2,1,0,3:T(1,128)S(1)}, f32[2,3,1,128,512]{4,2,1,0,3:T(1,128)S(1)}, u32[]{:S(2)}, u32[]{:S(2)}) collective-permute-start(f32[2,3,1,128,512]{4,2,1,0,3:T(1,128)S(1)} %get-tuple-element.23), channel_id=1, source_target_pairs={{0,1},{1,2},{2,3},{3,4},{4,5},{5,6},{6,7},{7,8},{8,9},{9,10},{10,1... | collective-permute-start | bytes 4718600 | tf_op jit(solution)/shard_map/ppermute | solution.py:17
  349.8 20.1 %collective-permute-start.12 = (f32[2,3,1,128,512]{4,2,1,0,3:T(1,128)}, f32[2,3,1,128,512]{4,2,1,0,3:T(1,128)}, u32[]{:S(2)}, u32[]{:S(2)}) collective-permute-start(f32[2,3,1,128,512]{4,2,1,0,3:T(1,128)} %get-tuple-element.14), channel_id=1, source_target_pairs={{1,0},{2,1},{3,2},{4,3},{5,4},{6,5},{7,6},{8,7},{9,8},{10,9},{11,1... | collective-permute-start | bytes 4718600 | tf_op jit(solution)/shard_map/ppermute | solution.py:20
  351.8 23.8 %collective-permute-start.13 = (f32[2,3,1,128,512]{4,2,1,0,3:T(1,128)S(1)}, f32[2,3,1,128,512]{4,2,1,0,3:T(1,128)S(1)}, u32[]{:S(2)}, u32[]{:S(2)}) collective-permute-start(f32[2,3,1,128,512]{4,2,1,0,3:T(1,128)S(1)} %get-tuple-element.15), channel_id=1, source_target_pairs={{0,1},{1,2},{2,3},{3,4},{4,5},{5,6},{6,7},{7,8},{8,9},{9,10},{10,1... | collective-permute-start | bytes 4718600 | tf_op jit(solution)/shard_map/ppermute | solution.py:17
  396.9 20.1 %collective-permute-start.14 = (f32[2,3,1,128,512]{4,2,1,0,3:T(1,128)}, f32[2,3,1,128,512]{4,2,1,0,3:T(1,128)}, u32[]{:S(2)}, u32[]{:S(2)}) collective-permute-start(f32[2,3,1,128,512]{4,2,1,0,3:T(1,128)} %get-tuple-element.6), channel_id=1, source_target_pairs={{1,0},{2,1},{3,2},{4,3},{5,4},{6,5},{7,6},{8,7},{9,8},{10,9},{11,1... | collective-permute-start | bytes 4718600 | tf_op jit(solution)/shard_map/ppermute | solution.py:20
  398.8 23.9 %collective-permute-start.15 = (f32[2,3,1,128,512]{4,2,1,0,3:T(1,128)S(1)}, f32[2,3,1,128,512]{4,2,1,0,3:T(1,128)S(1)}, u32[]{:S(2)}, u32[]{:S(2)}) collective-permute-start(f32[2,3,1,128,512]{4,2,1,0,3:T(1,128)S(1)} %get-tuple-element.7), channel_id=1, source_target_pairs={{0,1},{1,2},{2,3},{3,4},{4,5},{5,6},{6,7},{7,8},{8,9},{9,10},{10,1... | collective-permute-start | bytes 4718600 | tf_op jit(solution)/shard_map/ppermute | solution.py:17
  500.2 38.8 %all-to-all-start.1 = ((f32[16,3,2,16,512]{4,3,2,1,0:T(8,128)}), f32[16,3,2,16,512]{4,3,2,1,0:T(8,128)}, u32[]{:S(2)}, u32[]{:S(2)}) async-start(f32[16,3,2,16,512]{4,3,2,1,0:T(8,128)} %copy.54), calls=%async_computation.1 | async-start | bytes 6291456 | tf_op jit(solution)/shard_map/all_to_all | solution.py:71
  (9 other events, 16.8 us)
where the time goes:
time: 550 us; the launch traced here: 544 us
  local copies, waits for them, and re-layouts  165 us (30%)
  other arithmetic  134 us (24%)
  waiting for transfers between devices  123 us (22%)
  blocking collectives  72.8 us (13%)
  starting transfers between devices  42.3 us (8%)
    add x8, other arithmetic, relax_sweep(): return centre + RELAXATION * (weighted / weight - centre)  133 us
    ppermute x8, waiting for transfers between devices, padded_2(): lax.ppermute(lax.slice_in_dim(block, 0, width, axis=dim), axis, backward)  51.5 us
    slice x16, local copies, waits for them, and re-layouts, relax_sweep(): beside_all = jnp.roll(centre, 1, axis=4) + jnp.roll(centre, -1, axis=4)  50.6 us
    all_to_all x1, blocking collectives, per_device(): lax.all_to_all(displaced, 'inst', split_axis=3, concat_axis=0, tiled=True)  42.8 us
    ppermute x8, waiting for transfers between devices, padded_2(): lax.ppermute(lax.slice_in_dim(block, block.shape[dim] - width, None, axis...  39.3 us
    all_to_all x1, waiting for transfers between devices, per_device(): lax.all_to_all(time_rate, 'inst', split_axis=0, concat_axis=3, tiled=True)  31.7 us
    all_gather x1, blocking collectives, per_device(): full_surface = lax.all_gather(surface_disp, 'slab', axis=2, tiled=True)  30 us
    slice x9, local copies, waits for them, and re-layouts, padded_2(): lax.slice_in_dim(block, 0, width, axis=dim)  29.9 us
  transfers between devices with their start and end apart: 17, of which 15 were waited for; matrix products, arithmetic and copies ran while one was open for 21% of the time, Pallas kernels for 0%

commit v1 on v0

v1 whole, which is shorter than its diff:
```python
import math

import jax
import jax.numpy as jnp
from jax import lax
from jax.experimental import pallas as pl
from jax.experimental.pallas import tpu as pltpu
from jax.sharding import PartitionSpec as P

MESH = pl.DeviceIdType.MESH
SWEEPS = 8
ROWS = 48
INSTANCES = 16
GROUP = 8
INST_DEVICES = 8
CORE_ROWS = 32
SHARE = 16
LANES = 512


def rate_factor(d):
    return 2.0 * math.pi / INSTANCES * 0.5 * (-1.0) ** d / math.tan(math.pi * d / INSTANCES)


def window_start(row_block):
    return pl.multiple_of(
        32 * row_block - 8 + 8 * ((3 - row_block) // 3) - 8 * (row_block // 3), 8
    )


def kernel(
    prior, surface, springs, code,
    disp_out, vel_out,
    field, coef, own_springs, own_coef, disp, vel_in, rate, table, codes, wall, free,
    in_send, in_recv, coef_send, coef_recv, table_send, table_recv, code_send, code_recv,
    edge_send, edge_recv, out_send, out_recv, vin_send, vin_recv, vout_send, vout_recv,
    local_sem, disp_sem,
):
    inst = lax.axis_index("inst")
    slab = lax.axis_index("slab")
    half = slab // GROUP
    rank = slab % GROUP
    row_block = rank // 2
    core = rank % 2
    partner = (1 - half) * GROUP + rank
    edge = 16 - 15 * half
    step_dir = 2 * half - 1

    spring_load = pltpu.make_async_copy(springs, own_springs, local_sem.at[0])
    spring_load.start()

    barrier = pltpu.get_barrier_semaphore()
    for shift in range(1, 2 * GROUP):
        pl.semaphore_signal(
            barrier, inc=1, device_id=(inst, (slab + shift) % (2 * GROUP)), device_id_type=MESH
        )
    for shift in range(1, INST_DEVICES):
        pl.semaphore_signal(
            barrier, inc=1, device_id=((inst + shift) % INST_DEVICES, slab), device_id_type=MESH
        )
    pl.semaphore_wait(barrier, 2 * GROUP - 1 + INST_DEVICES - 1)

    def remote(src, dst, send, recv, device):
        return pltpu.make_async_remote_copy(
            src_ref=src, dst_ref=dst, send_sem=send, recv_sem=recv,
            device_id=device, device_id_type=MESH,
        )

    def wait_bytes(ref, sem):
        pltpu.make_async_copy(ref, ref, sem).wait()

    for to_half in range(2):
        for to_core in range(2):
            target = to_half * GROUP + to_core
            piece = table.at[:, pl.ds(pl.multiple_of(slab * 8, 8), 8), :]

            @pl.when(target != slab)
            def _():
                remote(surface.at[to_core], piece, table_send, table_recv, (inst, target)).start()

            @pl.when(target == slab)
            def _():
                pltpu.make_async_copy(surface.at[to_core], piece, table_recv).start()

    for to_core in range(2):
        target = half * GROUP + to_core

        @pl.when(target != slab)
        def _():
            remote(code, codes.at[rank], code_send, code_recv, (inst, target)).start()

        @pl.when(target == slab)
        def _():
            pltpu.make_async_copy(code, codes.at[rank], code_recv).start()

    def start_in(c):
        dst = field.at[0, c, pl.ds(1 + 2 * rank, 2)]
        pltpu.make_async_copy(
            prior.at[core, c, :, pl.ds(window_start(row_block), ROWS), :], dst, in_recv.at[c]
        ).start()
        for shift in range(1, GROUP):
            to = (rank + shift) % GROUP
            remote(
                prior.at[to % 2, c, :, pl.ds(window_start(to // 2), ROWS), :], dst,
                in_send.at[c], in_recv.at[c], (inst, half * GROUP + to),
            ).start()

    start_in(0)

    spring_load.wait()

    @pl.loop(0, 2)
    def _(p):
        @pl.loop(0, 16)
        def _(t):
            rows = pl.ds(pl.multiple_of(8 * t, 8), 8)
            s0 = own_springs[0, p, rows, :]
            s1 = own_springs[1, p, rows, :]
            s2 = own_springs[2, p, rows, :]
            scale = 0.45 / (s0 + s1 + s2)
            own_coef[0, p, rows, :] = s0 * scale
            own_coef[1, p, rows, :] = s1 * scale

    coef_dst = coef.at[:, pl.ds(2 * rank, 2)]
    pltpu.make_async_copy(
        own_coef.at[:, :, pl.ds(window_start(row_block), ROWS), :], coef_dst, coef_recv
    ).start()
    for shift in range(1, GROUP):
        to = (rank + shift) % GROUP
        remote(
            own_coef.at[:, :, pl.ds(window_start(to // 2), ROWS), :], coef_dst,
            coef_send, coef_recv, (inst, half * GROUP + to),
        ).start()

    start_in(1)
    start_in(2)

    zero = jnp.zeros((8, LANES), jnp.float32)

    @pl.loop(0, 6)
    def _(i):
        for t in range(ROWS // 8):
            field[i // 3, i % 3, 17 * half, 8 * t : 8 * t + 8, :] = zero

    @pl.loop(0, 16)
    def _(p):
        free[p] = zero
        for c in range(3):
            wall[c, p] = zero

    @pl.when(row_block == 0)
    def _():
        wait_bytes(table, table_recv)
        wait_bytes(codes, code_recv)
        low = [codes[s] & 127 for s in range(GROUP)]
        high = [codes[s] >> 7 for s in range(GROUP)]

        def pick(h, picked):
            hits = [high[s] == h for s in range(GROUP)]
            result = []
            for c in range(3):
                row = jnp.broadcast_to(table[c, pl.ds(h, 1), :], (8, 128))
                for s in range(GROUP):
                    value = jnp.take_along_axis(row, low[s], axis=1, mode="promise_in_bounds")
                    result.append(jnp.where(hits[s], value, picked[c * GROUP + s]))
            return tuple(result)

        picked = lax.fori_loop(
            0, 128, pick, tuple(jnp.zeros((8, 128), jnp.float32) for _ in range(3 * GROUP))
        )
        for s in range(GROUP):
            released = (codes[s] < 0).astype(jnp.float32)
            for row in range(8):
                lanes = slice(128 * (row % 4), 128 * (row % 4) + 128)
                free[2 * s + row // 4, 0:1, lanes] = released[row : row + 1, :]
                for c in range(3):
                    wall[c, 2 * s + row // 4, 0:1, lanes] = picked[c * GROUP + s][row : row + 1, :]

    row_index = lax.broadcasted_iota(jnp.int32, (8, LANES), 0)
    first = row_index == 0
    last = row_index == 7

    def relax_plane(c, now, later, p):
        tiles = ROWS // 8
        u = [field[now, c, p, 8 * t : 8 * t + 8, :] for t in range(tiles)]
        down = [pltpu.roll(v, 1, 0) for v in u]
        up = [pltpu.roll(v, 7, 0) for v in u]
        ghost = wall[c, p - 1, 0:1, :] + free[p - 1, 0:1, :] * u[0][0:1, :]
        for t in range(tiles):
            rows = slice(8 * t, 8 * t + 8)
            below = jnp.where(first, down[t - 1] if t else ghost, down[t])
            above = jnp.where(last, up[t + 1] if t + 1 < tiles else 0.0, up[t])
            beside = pltpu.roll(u[t], 1, 1) + pltpu.roll(u[t], LANES - 1, 1)
            planes = field[now, c, p - 1, rows, :] + field[now, c, p + 1, rows, :]
            field[later, c, p, rows, :] = (
                0.1 * u[t] + 0.45 * beside
                + coef[0, p - 1, rows, :] * (planes - beside)
                + coef[1, p - 1, rows, :] * ((below + above) - beside)
            )

    def edge_copy(c, slot):
        return remote(
            field.at[slot, c, edge], field.at[slot, c, 17 * half],
            edge_send.at[c, slot], edge_recv.at[c, slot], (inst, partner),
        )

    def sweep(c, s):
        now = s % 2
        later = 1 - now
        edge_copy(c, now).wait_recv()
        relax_plane(c, now, later, edge)

        @pl.when(s < SWEEPS - 1)
        def _():
            edge_copy(c, later).start()

        @pl.loop(1, 16)
        def _(i):
            relax_plane(c, now, later, edge + i * step_dir)

        edge_copy(c, now).wait_send()

    def begin_sweeps(c):
        wait_bytes(field.at[0, c, pl.ds(1, 16)], in_recv.at[c])
        edge_copy(c, 0).start()

    def sweeps(c, low, high):
        @pl.loop(low, high)
        def _(s):
            sweep(c, s)

    own_rows = pl.multiple_of(32 * row_block - window_start(row_block), 8)

    def start_out(c):
        dst = disp.at[core, c, :, pl.ds(pl.multiple_of(CORE_ROWS * row_block, 8), CORE_ROWS), :]
        pltpu.make_async_copy(
            field.at[0, c, pl.ds(1 + 2 * rank, 2), pl.ds(own_rows, CORE_ROWS), :],
            dst, out_recv.at[c],
        ).start()
        for shift in range(1, GROUP):
            to = (rank + shift) % GROUP
            remote(
                field.at[0, c, pl.ds(1 + 2 * to, 2), pl.ds(own_rows, CORE_ROWS), :], dst,
                out_send.at[c], out_recv.at[c], (inst, half * GROUP + to),
            ).start()

    def disp_copy(c):
        return pltpu.make_async_copy(disp.at[:, c], disp_out.at[:, c], disp_sem.at[c])

    def start_vin(c):
        wait_bytes(disp.at[:, c], out_recv.at[c])
        dst = vel_in.at[pl.ds(2 * inst, 2), c]
        for shift in range(1, INST_DEVICES):
            to = (inst + shift) % INST_DEVICES
            remote(
                disp.at[:, c, :, pl.ds(pl.multiple_of(SHARE * to, 8), SHARE), :], dst,
                vin_send.at[c], vin_recv.at[c], (to, slab),
            ).start()
        pltpu.make_async_copy(
            disp.at[:, c, :, pl.ds(pl.multiple_of(SHARE * inst, 8), SHARE), :], dst, vin_recv.at[c]
        ).start()
        disp_copy(c).start()

    def start_vout(c):
        wait_bytes(vel_in.at[:, c], vin_recv.at[c])

        @pl.loop(0, 4)
        def _(i):
            rows = pl.ds(pl.multiple_of(8 * (i % 2), 8), 8)
            for lane in range(0, LANES, 128):
                lanes = slice(lane, lane + 128)
                u = [vel_in[n, c, i // 2, rows, lanes] for n in range(INSTANCES)]
                for n in range(INSTANCES):
                    total = None
                    for d in range(1, 8):
                        term = rate_factor(d) * (u[(n - d) % INSTANCES] - u[(n + d) % INSTANCES])
                        total = term if total is None else total + term
                    rate[n, c, i // 2, rows, lanes] = total

        dst = vel_out.at[:, c, :, pl.ds(pl.multiple_of(SHARE * inst, 8), SHARE), :]
        for shift in range(1, INST_DEVICES):
            to = (inst + shift) % INST_DEVICES
            remote(
                rate.at[pl.ds(2 * to, 2), c], dst,
                vout_send.at[c], vout_recv.at[c], (to, slab),
            ).start()
        pltpu.make_async_copy(rate.at[pl.ds(2 * inst, 2), c], dst, vout_recv.at[c]).start()

    wait_bytes(coef, coef_recv)
    begin_sweeps(0)
    sweeps(0, 0, SWEEPS)
    start_out(0)
    begin_sweeps(1)
    sweeps(1, 0, 4)
    start_vin(0)
    sweeps(1, 4, SWEEPS)
    start_out(1)
    begin_sweeps(2)
    start_vout(0)
    sweeps(2, 0, 4)
    start_vin(1)
    sweeps(2, 4, SWEEPS)
    start_out(2)
    start_vout(1)
    start_vin(2)
    start_vout(2)

    for c in range(3):
        disp_copy(c).wait()
        wait_bytes(vel_out.at[:, c], vout_recv.at[c])
        wait_bytes(field.at[0, c, pl.ds(1, 14)], in_send.at[c])
        wait_bytes(field.at[0, c, pl.ds(1, 14), pl.ds(0, CORE_ROWS), :], out_send.at[c])
        wait_bytes(vel_in.at[pl.ds(0, 14), c], vin_send.at[c])
        wait_bytes(rate.at[pl.ds(0, 14), c], vout_send.at[c])
    wait_bytes(coef.at[:, pl.ds(0, 14)], coef_send)
    wait_bytes(table.at[:, pl.ds(0, 24)], table_send)
    wait_bytes(codes.at[0], code_send)

    @pl.when(row_block != 0)
    def _():
        wait_bytes(table.at[:, pl.ds(0, 8)], table_send)
        wait_bytes(codes.at[0], code_send)


def per_device(prior_disp, surface_disp, springs, wall_row, wall_mask):
    surface = surface_disp.reshape(2, 3, 8, 128)
    code = jnp.where(wall_mask != 0, wall_row, -1).reshape(8, 128)
    f32 = jnp.float32
    dma = pltpu.SemaphoreType.DMA
    shape = jax.ShapeDtypeStruct(prior_disp.shape, f32)
    return pl.pallas_call(
        kernel,
        out_shape=(shape, shape),
        in_specs=[pl.BlockSpec(memory_space=pl.ANY)] * 4,
        out_specs=(pl.BlockSpec(memory_space=pl.ANY),) * 2,
        scratch_shapes=[
            pltpu.VMEM((2, 3, 18, ROWS, LANES), f32),
            pltpu.VMEM((2, 16, ROWS, LANES), f32),
            pltpu.VMEM((3, 2, 128, LANES), f32),
            pltpu.VMEM((2, 2, 128, LANES), f32),
            pltpu.VMEM((2, 3, 2, 128, LANES), f32),
            pltpu.VMEM((INSTANCES, 3, 2, SHARE, LANES), f32),
            pltpu.VMEM((INSTANCES, 3, 2, SHARE, LANES), f32),
            pltpu.VMEM((3, 128, 128), f32),
            pltpu.VMEM((GROUP, 8, 128), jnp.int32),
            pltpu.VMEM((3, 16, 8, LANES), f32),
            pltpu.VMEM((16, 8, LANES), f32),
            dma((3,)), dma((3,)), dma, dma, dma, dma, dma, dma,
            dma((3, 2)), dma((3, 2)), dma((3,)), dma((3,)), dma((3,)), dma((3,)),
            dma((3,)), dma((3,)),
            dma((1,)), dma((3,)),
        ],
        compiler_params=pltpu.CompilerParams(
            collective_id=0, has_side_effects=True, vmem_limit_bytes=48 * 1024 * 1024
        ),
    )(prior_disp, surface, springs, code)


def solution(mesh):
    in_specs = (
        P("inst", None, "slab", None, None),
        P("inst", None, "slab"),
        P(None, "slab", None, None),
        P("slab", None),
        P("slab", None),
    )
    out_specs = (P("inst", None, "slab", None, None), P("inst", None, "slab", None, None))
    return jax.shard_map(
        per_device, mesh=mesh, in_specs=in_specs, out_specs=out_specs, check_vma=False
    )
```

time: 550 us -> 235 us (0.43); the launches traced: 544 us -> 234 us
  Pallas kernels: 0 us -> 226 us
  local copies, waits for them, and re-layouts: 165 us -> 6.86 us
  other arithmetic: 134 us -> 0.71 us
  waiting for transfers between devices: 123 us -> 0 us
  blocking collectives: 72.8 us -> 0 us
  starting transfers between devices: 42.3 us -> 0 us
    pallas_call x0 -> x1, Pallas kernels: none -> 226 us  [per_device(): pl.pallas_call(kernel, out_shape=(shape, shape), in_specs=[pl.BlockSpec(m...]
    add x16 -> x0, other arithmetic: 133 us -> none  [the longest x8 133 us: relax_sweep(): return centre + RELAXATION * (weighted / weight - centre)]
    slice x34 -> x0, local copies, waits for them, and re-layouts: 99.6 us -> none  [the longest x16 50.6 us: relax_sweep(): beside_all = jnp.roll(centre, 1, axis=4) + jnp.roll(centre, -1, axis=4)]
    ppermute x16 -> x0, waiting for transfers between devices: 90.9 us -> none  [the longest x8 51.5 us: padded_2(): lax.ppermute(lax.slice_in_dim(block, 0, width, axis=dim), axis, backward)]
    all_to_all x1 -> x0, blocking collectives: 42.8 us -> none  [per_device(): lax.all_to_all(displaced, 'inst', split_axis=3, concat_axis=0, tiled=True)]
    ppermute x16 -> x0, starting transfers between devices: 37.8 us -> none  [the longest x8 20.5 us: padded_2(): lax.ppermute(lax.slice_in_dim(block, block.shape[dim] - width, None, axis...]
    all_to_all x1 -> x0, waiting for transfers between devices: 31.7 us -> none  [per_device(): lax.all_to_all(time_rate, 'inst', split_axis=0, concat_axis=3, tiled=True)]
    all_gather x1 -> x0, blocking collectives: 30 us -> none  [per_device(): full_surface = lax.all_gather(surface_disp, 'slab', axis=2, tiled=True)]
  transfers between devices with their start and end apart: 17 -> 0, of which waited for: 15 -> 0; matrix products, arithmetic and copies ran while one was open for 21% -> 0% of each run, Pallas kernels for 0% -> 0%
where the time goes in v1:
time: 235 us; the launch traced here: 234 us
  Pallas kernels  226 us (96%)
  local copies, waits for them, and re-layouts  6.86 us (3%)
    pallas_call x1, Pallas kernels, per_device(): pl.pallas_call(kernel, out_shape=(shape, shape), in_specs=[pl.BlockSpec(m...  226 us
    unnamed x6, local copies, waits for them, and re-layouts  6.08 us

profile of v1, /device:TPU:32, one launch (start us, length us, event | category | flops | bytes accessed | tf_op | source)
XLA Modules:
  0.0 234.3 jit_solution(15924902530215718898)
XLA Ops:
  0.6 0.7 compare_select_fusion
  1.4 0.8 reshape.10
  2.1 0.0 copy-start
  2.1 1.4 copy-done
  3.5 226.1 %shard_map.68 = (f32[2,3,2,128,512]{4,3,2,1,0:T(8,128)S(1)}, f32[2,3,2,128,512]{4,3,2,1,0:T(8,128)}) custom-call(f32[2,3,2,128,512]{4,3,2,1,0:T(8,128)} %prior.1, f32[2,3,8,128]{3,2,1,0:T(8,128)S(1)} %copy.8.surface, f32[3,2,128,512]{3,2,1,0:T(8,128)S(1)} %copy-done, s32[8,128]{1,0:T(8,128)S(1)} %reshape.11.code), custom_call_target="tpu_custom_call" | custom-call | tf_op jit(solution)/shard_map/pallas_call | solution.py:331
  229.6 0.0 copy-start.1
  229.6 1.7 copy.11
  231.3 1.3 copy-done.1
  232.6 1.7 copy.12
  (2 shorter events, 0.0 us)
Async XLA Ops:
  2.1 1.4 copy-start
  229.6 3.0 %copy-start.1 = (f32[2,3,2,128,512]{4,3,2,1,0:T(8,128)S(1)}, f32[2,3,2,128,512]{4,3,2,1,0:T(8,128)}, u32[]{:S(2)}) copy-start(f32[2,3,2,128,512]{4,3,2,1,0:T(8,128)} %get-tuple-element.5) | copy-start | bytes 9437188

commit v2 on v1

v2 whole, which is shorter than its diff:
```python
import math

import jax
import jax.numpy as jnp
from jax import lax
from jax.experimental import pallas as pl
from jax.experimental.pallas import tpu as pltpu
from jax.sharding import PartitionSpec as P

MESH = pl.DeviceIdType.MESH
SWEEPS = 8
ROWS = 72
CORE_PLANES = 8
INSTANCES = 16
GROUP = 8
INST_DEVICES = 8
CORE_ROWS = 64
PIECES = 3
PIECE_ROWS = 24
DIRECT = 24
SHARE = 16
LANES = 512


def rate_factor(d):
    return 2.0 * math.pi / INSTANCES * 0.5 * (-1.0) ** d / math.tan(math.pi * d / INSTANCES)


INST_ORDER = (1, 3, 4, 7, 2, 5, 6)


def window(row_block, first=0, count=ROWS):
    return pl.ds(pl.multiple_of(56 * (row_block % 2) + first, 8), count)


def inst_partner(inst, offset):
    return (inst // 4 + offset // 4) % 2 * 4 + (inst + offset) % 4


def kernel(
    prior, surface, springs, code,
    disp, vel_out,
    field, coef, own_coef, vel_in, rate, table, codes, wall, free,
    in_send, in_recv, coef_send, coef_recv, part_send, part_recv, share_send, share_recv, table_send, table_recv, code_send, code_recv,
    edge_send, edge_recv, out_send, out_recv, vin_send, vin_recv, vout_send, vout_recv,
):
    inst = lax.axis_index("inst")
    slab = lax.axis_index("slab")
    half = slab // GROUP
    rank = slab % GROUP
    row_block = rank // 2
    core = rank % 2
    own_inst = row_block // 2
    chain = 2 * half + core

    barrier = pltpu.get_barrier_semaphore()
    for shift in range(1, 2 * GROUP):
        pl.semaphore_signal(
            barrier, inc=1, device_id=(inst, (slab + shift) % (2 * GROUP)), device_id_type=MESH
        )
    for shift in range(1, INST_DEVICES):
        pl.semaphore_signal(
            barrier, inc=1, device_id=((inst + shift) % INST_DEVICES, slab), device_id_type=MESH
        )
    pl.semaphore_wait(barrier, 2 * GROUP - 1 + INST_DEVICES - 1)

    def remote(src, dst, send, recv, device):
        return pltpu.make_async_remote_copy(
            src_ref=src, dst_ref=dst, send_sem=send, recv_sem=recv,
            device_id=device, device_id_type=MESH,
        )

    def wait_bytes(ref, sem):
        pltpu.make_async_copy(ref, ref, sem).wait()

    def table_sends(action):
        for n in range(2):
            for k in range(4):
                target = k // 2 * GROUP + 4 * n + k % 2
                action(surface.at[n], table.at[:, pl.ds(pl.multiple_of(slab * 8, 8), 8), :],
                       table_send, table_recv, target)

    def code_sends(action):
        for n in range(2):
            action(code, codes.at[rank % 4], code_send, code_recv,
                   half * GROUP + 4 * n + row_block // 2)

    def start_either(src, dst, send, recv, target):
        @pl.when(target != slab)
        def _():
            remote(src, dst, send, recv, (inst, target)).start()

        @pl.when(target == slab)
        def _():
            pltpu.make_async_copy(src, dst, recv).start()

    def finish_either(src, dst, send, recv, target):
        @pl.when(target != slab)
        def _():
            remote(src, dst, send, recv, (inst, target)).wait_send()

    def row_sends(action, source, dst, send, recv):
        for shift in (0, 1, 3, 2):
            to = (row_block + shift) % 4
            action(source(to), dst, send, recv, half * GROUP + 2 * to + row_block // 2)

    def in_sends(action, c):
        row_sends(action, lambda to: prior.at[to // 2, c, :, window(to), :],
                  field.at[0, c, pl.ds(1 + 2 * (rank % 4), 2)], in_send.at[c], in_recv.at[c])

    quarter = inst % 4
    shared = pl.ds(DIRECT, ROWS - DIRECT)

    def coef_sends(action):
        row_sends(action, lambda to: own_coef.at[:, window(to, 0, DIRECT), :],
                  coef.at[:, rank % 4, pl.ds(0, DIRECT)], coef_send, coef_recv)

    def part_sends(action):
        row_sends(action, lambda to: own_coef.at[quarter, window(to, DIRECT, ROWS - DIRECT), :],
                  coef.at[quarter, rank % 4, shared], part_send, part_recv)

    def start_in(c):
        in_sends(start_either, c)

    @pl.loop(0, 32)
    def _(i):
        p = i // 16
        rows = pl.ds(pl.multiple_of(8 * (i % 16), 8), 8)
        s0 = springs[0, p, rows, :]
        s1 = springs[1, p, rows, :]
        s2 = springs[2, p, rows, :]
        scale = 0.45 / (s0 + s1 + s2)
        own_coef[p, rows, :] = s0 * scale
        own_coef[2 + p, rows, :] = s1 * scale

    part_sends(start_either)
    table_sends(start_either)
    code_sends(start_either)
    start_in(0)
    coef_sends(start_either)

    wait_bytes(coef.at[0, :, shared], part_recv)
    for offset in (1, 3, 2):
        mine = coef.at[quarter, :, shared]
        remote(
            mine, mine, share_send, share_recv, (inst // 4 * 4 + (inst + offset) % 4, slab)
        ).start()

    zero = jnp.zeros((8, LANES), jnp.float32)

    @pl.loop(0, 6)
    def _(i):
        for t in range(ROWS // 8):
            rows = slice(8 * t, 8 * t + 8)

            @pl.when(chain == 0)
            def _():
                field[i // 3, i % 3, 0, rows, :] = zero

            @pl.when(chain == 3)
            def _():
                field[i // 3, i % 3, CORE_PLANES + 1, rows, :] = zero

    @pl.loop(0, CORE_PLANES)
    def _(p):
        free[p] = zero
        for c in range(3):
            wall[c, p] = zero

    @pl.when(row_block % 2 == 0)
    def _():
        wait_bytes(table, table_recv)
        wait_bytes(codes, code_recv)
        low = [codes[s] & 127 for s in range(4)]
        high = [codes[s] >> 7 for s in range(4)]

        def pick(h, picked):
            hits = [high[s] == h for s in range(4)]
            result = []
            for c in range(3):
                row = jnp.broadcast_to(table[c, pl.ds(h, 1), :], (8, 128))
                for s in range(4):
                    value = jnp.take_along_axis(row, low[s], axis=1, mode="promise_in_bounds")
                    result.append(jnp.where(hits[s], value, picked[c * 4 + s]))
            return tuple(result)

        picked = lax.fori_loop(
            0, 128, pick, tuple(jnp.zeros((8, 128), jnp.float32) for _ in range(12))
        )
        for s in range(4):
            released = (codes[s] < 0).astype(jnp.float32)
            for row in range(8):
                lanes = slice(128 * (row % 4), 128 * (row % 4) + 128)
                free[2 * s + row // 4, 0:1, lanes] = released[row : row + 1, :]
                for c in range(3):
                    wall[c, 2 * s + row // 4, 0:1, lanes] = picked[c * 4 + s][row : row + 1, :]

    row_index = lax.broadcasted_iota(jnp.int32, (8, LANES), 0)
    first = row_index == 0
    last = row_index == 7

    def relax_plane(c, now, later, p, piece=None):
        tiles = ROWS // 8
        per = PIECE_ROWS // 8
        wanted = range(tiles) if piece is None else range(piece * per, piece * per + per)
        near = range(max(wanted[0] - 1, 0), min(wanted[-1] + 2, tiles))
        u = {t: field[now, c, p, 8 * t : 8 * t + 8, :] for t in near}
        down = {t: pltpu.roll(u[t], 1, 0) for t in near}
        up = {t: pltpu.roll(u[t], 7, 0) for t in near}
        if 0 in u:
            ghost = wall[c, p - 1, 0:1, :] + free[p - 1, 0:1, :] * u[0][0:1, :]
        for t in wanted:
            rows = slice(8 * t, 8 * t + 8)
            below = jnp.where(first, down[t - 1] if t else ghost, down[t])
            above = jnp.where(last, up[t + 1] if t + 1 < tiles else 0.0, up[t])
            beside = pltpu.roll(u[t], 1, 1) + pltpu.roll(u[t], LANES - 1, 1)
            planes = field[now, c, p - 1, rows, :] + field[now, c, p + 1, rows, :]
            field[later, c, p, rows, :] = (
                0.1 * u[t] + 0.45 * beside
                + coef[(p - 1) % 2, (p - 1) // 2, rows, :] * (planes - beside)
                + coef[2 + (p - 1) % 2, (p - 1) // 2, rows, :] * ((below + above) - beside)
            )

    def piece_rows(piece):
        return pl.ds(piece * PIECE_ROWS, PIECE_ROWS)

    def edge_copy(c, now, upper, piece):
        to = (chain + (1 if upper else 3)) % 4
        target = to // 2 * GROUP + 2 * row_block + to % 2
        src, dst = (CORE_PLANES, 0) if upper else (1, CORE_PLANES + 1)
        return remote(
            field.at[now, c, src, piece_rows(piece)], field.at[now, c, dst, piece_rows(piece)],
            edge_send.at[c, now, upper, piece], edge_recv.at[c, now, 1 - upper, piece],
            (inst, target),
        )

    has = (chain > 0, chain < 3)

    def sweep(c, s):
        now = s % 2
        later = 1 - now
        for piece in range(PIECES):
            for upper in range(2):
                @pl.when(has[upper])
                def _():
                    wait_bytes(
                        field.at[now, c, 0, piece_rows(piece)], edge_recv.at[c, now, upper, piece]
                    )

                relax_plane(c, now, later, CORE_PLANES if upper else 1, piece)

                @pl.when(has[upper] & (s < SWEEPS - 1))
                def _():
                    edge_copy(c, later, upper, piece).start()

        @pl.loop(2, CORE_PLANES)
        def _(p):
            relax_plane(c, now, later, p)

        for upper in range(2):
            @pl.when(has[upper])
            def _():
                for piece in range(PIECES):
                    edge_copy(c, now, upper, piece).wait_send()

    def begin_sweeps(c):
        wait_bytes(field.at[0, c, pl.ds(1, CORE_PLANES)], in_recv.at[c])
        for upper in range(2):
            @pl.when(has[upper])
            def _():
                for piece in range(PIECES):
                    edge_copy(c, 0, upper, piece).start()

    def sweeps(count, *parts):
        @pl.loop(0, count)
        def _(s):
            for c, first_sweep in parts:
                sweep(c, first_sweep + s)

    def out_sends(action, c):
        own_rows = pl.ds(pl.multiple_of(8 * (row_block % 2), 8), CORE_ROWS)
        dst = disp.at[
            own_inst, c, :, pl.ds(pl.multiple_of(CORE_ROWS * (row_block % 2), 8), CORE_ROWS), :
        ]
        for shift in range(4):
            to = (rank + shift) % 4
            action(
                field.at[0, c, pl.ds(1 + 2 * to, 2), own_rows, :], dst,
                out_send.at[c], out_recv.at[c], half * GROUP + 4 * core + to,
            )

    def start_out(c):
        out_sends(start_either, c)

    def start_vin(c):
        wait_bytes(disp.at[:, c], out_recv.at[c])
        dst = vel_in.at[pl.ds(2 * inst, 2), c]
        for offset in INST_ORDER:
            to = inst_partner(inst, offset)
            remote(
                disp.at[:, c, :, pl.ds(pl.multiple_of(SHARE * to, 8), SHARE), :], dst,
                vin_send.at[c], vin_recv.at[c], (to, slab),
            ).start()
        pltpu.make_async_copy(
            disp.at[:, c, :, pl.ds(pl.multiple_of(SHARE * inst, 8), SHARE), :], dst, vin_recv.at[c]
        ).start()

    def start_vout(c):
        wait_bytes(vel_in.at[:, c], vin_recv.at[c])

        @pl.loop(0, 4)
        def _(i):
            rows = pl.ds(pl.multiple_of(8 * (i % 2), 8), 8)
            for lane in range(0, LANES, 128):
                lanes = slice(lane, lane + 128)
                u = [vel_in[n, c, i // 2, rows, lanes] for n in range(INSTANCES)]
                for n in range(INSTANCES):
                    total = None
                    for d in range(1, 8):
                        term = rate_factor(d) * (u[(n - d) % INSTANCES] - u[(n + d) % INSTANCES])
                        total = term if total is None else total + term
                    rate[n, c, i // 2, rows, lanes] = total

        dst = vel_out.at[:, c, :, pl.ds(pl.multiple_of(SHARE * inst, 8), SHARE), :]
        for offset in INST_ORDER:
            to = inst_partner(inst, offset)
            remote(
                rate.at[pl.ds(2 * to, 2), c], dst,
                vout_send.at[c], vout_recv.at[c], (to, slab),
            ).start()
        pltpu.make_async_copy(rate.at[pl.ds(2 * inst, 2), c], dst, vout_recv.at[c]).start()

    wait_bytes(coef.at[:, :, pl.ds(0, DIRECT)], coef_recv)
    wait_bytes(coef.at[pl.ds(0, 3), :, shared], share_recv)
    begin_sweeps(0)
    start_in(1)
    sweeps(4, (0, 0))
    begin_sweeps(1)
    start_in(2)
    sweeps(4, (0, 4), (1, 0))
    start_out(0)
    begin_sweeps(2)
    sweeps(2, (1, 4), (2, 0))
    start_vin(0)
    sweeps(2, (1, 6), (2, 2))
    start_out(1)
    sweeps(4, (2, 4))
    start_out(2)
    start_vin(1)
    start_vout(0)
    start_vin(2)
    start_vout(1)
    start_vout(2)

    for c in range(3):
        wait_bytes(vel_out.at[:, c], vout_recv.at[c])
        in_sends(finish_either, c)
        out_sends(finish_either, c)
        wait_bytes(vel_in.at[pl.ds(0, 14), c], vin_send.at[c])
        wait_bytes(rate.at[pl.ds(0, 14), c], vout_send.at[c])
    wait_bytes(coef.at[pl.ds(0, 3), :, shared], share_send)
    coef_sends(finish_either)
    part_sends(finish_either)
    table_sends(finish_either)
    code_sends(finish_either)


def per_device(prior_disp, surface_disp, springs, wall_row, wall_mask):
    surface = surface_disp.reshape(2, 3, 8, 128)
    code = jnp.where(wall_mask != 0, wall_row, -1).reshape(8, 128)
    f32 = jnp.float32
    dma = pltpu.SemaphoreType.DMA
    shape = jax.ShapeDtypeStruct(prior_disp.shape, f32)
    return pl.pallas_call(
        kernel,
        out_shape=(shape, shape),
        in_specs=[
            pl.BlockSpec(memory_space=pl.ANY),
            pl.BlockSpec(memory_space=pl.ANY),
            pl.BlockSpec(memory_space=pltpu.VMEM),
            pl.BlockSpec(memory_space=pl.ANY),
        ],
        out_specs=(pl.BlockSpec(memory_space=pltpu.VMEM),) * 2,
        scratch_shapes=[
            pltpu.VMEM((2, 3, CORE_PLANES + 2, ROWS, LANES), f32),
            pltpu.VMEM((4, CORE_PLANES // 2, ROWS, LANES), f32),
            pltpu.VMEM((4, 128, LANES), f32),
            pltpu.VMEM((INSTANCES, 3, 2, SHARE, LANES), f32),
            pltpu.VMEM((INSTANCES, 3, 2, SHARE, LANES), f32),
            pltpu.VMEM((3, 128, 128), f32),
            pltpu.VMEM((4, 8, 128), jnp.int32),
            pltpu.VMEM((3, CORE_PLANES, 8, LANES), f32),
            pltpu.VMEM((CORE_PLANES, 8, LANES), f32),
            dma((3,)), dma((3,)), dma, dma, dma, dma, dma, dma, dma, dma, dma, dma,
            dma((3, 2, 2, PIECES)), dma((3, 2, 2, PIECES)), dma((3,)), dma((3,)), dma((3,)), dma((3,)),
            dma((3,)), dma((3,)),
        ],
        compiler_params=pltpu.CompilerParams(
            collective_id=0, has_side_effects=True, vmem_limit_bytes=48 * 1024 * 1024
        ),
    )(prior_disp, surface, springs, code)


def solution(mesh):
    in_specs = (
        P("inst", None, "slab", None, None),
        P("inst", None, "slab"),
        P(None, "slab", None, None),
        P("slab", None),
        P("slab", None),
    )
    out_specs = (P("inst", None, "slab", None, None), P("inst", None, "slab", None, None))
    return jax.shard_map(
        per_device, mesh=mesh, in_specs=in_specs, out_specs=out_specs, check_vma=False
    )
```

time: 235 us -> 178 us (0.76)
  Pallas kernels: 226 us -> 168 us
    pallas_call x1, Pallas kernels: 226 us -> 168 us  [per_device(): pl.pallas_call(kernel, out_shape=(shape, shape), in_specs=[pl.BlockSpec(m...]
where the time goes in v2:
time: 178 us; the launch traced here: 176 us
  Pallas kernels  168 us (94%)
  local copies, waits for them, and re-layouts  6.86 us (4%)
    pallas_call x1, Pallas kernels, per_device(): pl.pallas_call(kernel, out_shape=(shape, shape), in_specs=[pl.BlockSpec(m...  168 us
    unnamed x6, local copies, waits for them, and re-layouts  6.08 us

profile of v2, /device:TPU:32, one launch (start us, length us, event | category | flops | bytes accessed | tf_op | source)
XLA Modules:
  0.0 176.1 jit_solution(2355271791728596144)
XLA Ops:
  0.6 0.7 compare_select_fusion
  1.4 0.8 reshape.10
  2.1 0.0 copy-start
  2.1 1.4 copy-done
  3.5 167.9 %shard_map.68 = (f32[2,3,2,128,512]{4,3,2,1,0:T(8,128)S(1)}, f32[2,3,2,128,512]{4,3,2,1,0:T(8,128)}) custom-call(f32[2,3,2,128,512]{4,3,2,1,0:T(8,128)} %prior.1, f32[2,3,8,128]{3,2,1,0:T(8,128)S(1)} %copy.8.surface, f32[3,2,128,512]{3,2,1,0:T(8,128)S(1)} %copy-done, s32[8,128]{1,0:T(8,128)S(1)} %reshape.11.code), custom_call_target="tpu_custom_call" | custom-call | tf_op jit(solution)/shard_map/pallas_call | solution.py:374
  171.4 0.0 copy-start.1
  171.4 1.7 copy.11
  173.1 1.3 copy-done.1
  174.4 1.7 copy.12
  (2 shorter events, 0.0 us)
Async XLA Ops:
  2.1 1.4 copy-start
  171.4 3.0 %copy-start.1 = (f32[2,3,2,128,512]{4,3,2,1,0:T(8,128)S(1)}, f32[2,3,2,128,512]{4,3,2,1,0:T(8,128)}, u32[]{:S(2)}) copy-start(f32[2,3,2,128,512]{4,3,2,1,0:T(8,128)} %get-tuple-element.5) | copy-start | bytes 9437188

commit v3 on v2

--- a/solution.py
+++ b/solution.py
@@ -17,7 +17,7 @@
 CORE_ROWS = 64
 PIECES = 3
 PIECE_ROWS = 24
-DIRECT = 24
+DIRECT = 16
 SHARE = 16
 LANES = 512
 
@@ -292,43 +292,46 @@
     def start_out(c):
         out_sends(start_either, c)
 
+    def share(of):
+        return pl.ds(pl.multiple_of(SHARE * of, 8), SHARE)
+
+    def inst_sends(source, own, dst, send, recv):
+        for offset in INST_ORDER:
+            to = inst_partner(inst, offset)
+            remote(source(to), dst, send, recv, (to, slab)).start()
+        pltpu.make_async_copy(own, dst, recv).start()
+
     def start_vin(c):
         wait_bytes(disp.at[:, c], out_recv.at[c])
-        dst = vel_in.at[pl.ds(2 * inst, 2), c]
-        for offset in INST_ORDER:
-            to = inst_partner(inst, offset)
-            remote(
-                disp.at[:, c, :, pl.ds(pl.multiple_of(SHARE * to, 8), SHARE), :], dst,
-                vin_send.at[c], vin_recv.at[c], (to, slab),
-            ).start()
-        pltpu.make_async_copy(
-            disp.at[:, c, :, pl.ds(pl.multiple_of(SHARE * inst, 8), SHARE), :], dst, vin_recv.at[c]
-        ).start()
+        for p in range(2):
+            inst_sends(
+                lambda to: disp.at[:, c, p, share(to), :], disp.at[:, c, p, share(inst), :],
+                vel_in.at[pl.ds(2 * inst, 2), c, p], vin_send.at[c, p], vin_recv.at[c, p],
+            )
 
     def start_vout(c):
-        wait_bytes(vel_in.at[:, c], vin_recv.at[c])
-
-        @pl.loop(0, 4)
-        def _(i):
-            rows = pl.ds(pl.multiple_of(8 * (i % 2), 8), 8)
-            for lane in range(0, LANES, 128):
-                lanes = slice(lane, lane + 128)
-                u = [vel_in[n, c, i // 2, rows, lanes] for n in range(INSTANCES)]
-                for n in range(INSTANCES):
-                    total = None
-                    for d in range(1, 8):
-                        term = rate_factor(d) * (u[(n - d) % INSTANCES] - u[(n + d) % INSTANCES])
-                        total = term if total is None else total + term
-                    rate[n, c, i // 2, rows, lanes] = total
-
-        dst = vel_out.at[:, c, :, pl.ds(pl.multiple_of(SHARE * inst, 8), SHARE), :]
-        for offset in INST_ORDER:
-            to = inst_partner(inst, offset)
-            remote(
-                rate.at[pl.ds(2 * to, 2), c], dst,
-                vout_send.at[c], vout_recv.at[c], (to, slab),
-            ).start()
-        pltpu.make_async_copy(rate.at[pl.ds(2 * inst, 2), c], dst, vout_recv.at[c]).start()
+        for p in range(2):
+            wait_bytes(vel_in.at[:, c, p], vin_recv.at[c, p])
+
+            @pl.loop(0, 2)
+            def _(i):
+                rows = pl.ds(pl.multiple_of(8 * i, 8), 8)
+                for lane in range(0, LANES, 128):
+                    lanes = slice(lane, lane + 128)
+                    u = [vel_in[n, c, p, rows, lanes] for n in range(INSTANCES)]
+                    for n in range(INSTANCES):
+                        total = None
+                        for d in range(1, 8):
+                            term = rate_factor(d) * (
+                                u[(n - d) % INSTANCES] - u[(n + d) % INSTANCES]
+                            )
+                            total = term if total is None else total + term
+                        rate[n, c, p, rows, lanes] = total
+
+            inst_sends(
+                lambda to: rate.at[pl.ds(2 * to, 2), c, p], rate.at[pl.ds(2 * inst, 2), c, p],
+                vel_out.at[:, c, p, share(inst), :], vout_send.at[c, p], vout_recv.at[c, p],
+            )
 
     wait_bytes(coef.at[:, :, pl.ds(0, DIRECT)], coef_recv)
     wait_bytes(coef.at[pl.ds(0, 3), :, shared], share_recv)
@@ -353,11 +356,12 @@
     start_vout(2)
 
     for c in range(3):
-        wait_bytes(vel_out.at[:, c], vout_recv.at[c])
         in_sends(finish_either, c)
         out_sends(finish_either, c)
-        wait_bytes(vel_in.at[pl.ds(0, 14), c], vin_send.at[c])
-        wait_bytes(rate.at[pl.ds(0, 14), c], vout_send.at[c])
+        for p in range(2):
+            wait_bytes(vel_out.at[:, c, p], vout_recv.at[c, p])
+            wait_bytes(vel_in.at[pl.ds(0, 14), c, p], vin_send.at[c, p])
+            wait_bytes(rate.at[pl.ds(0, 14), c, p], vout_send.at[c, p])
     wait_bytes(coef.at[pl.ds(0, 3), :, shared], share_send)
     coef_sends(finish_either)
     part_sends(finish_either)
@@ -392,11 +396,11 @@
             pltpu.VMEM((3, CORE_PLANES, 8, LANES), f32),
             pltpu.VMEM((CORE_PLANES, 8, LANES), f32),
             dma((3,)), dma((3,)), dma, dma, dma, dma, dma, dma, dma, dma, dma, dma,
-            dma((3, 2, 2, PIECES)), dma((3, 2, 2, PIECES)), dma((3,)), dma((3,)), dma((3,)), dma((3,)),
-            dma((3,)), dma((3,)),
+            dma((3, 2, 2, PIECES)), dma((3, 2, 2, PIECES)), dma((3,)), dma((3,)), dma((3, 2)), dma((3, 2)),
+            dma((3, 2)), dma((3, 2)),
         ],
         compiler_params=pltpu.CompilerParams(
-            collective_id=0, has_side_effects=True, vmem_limit_bytes=48 * 1024 * 1024
+            collective_id=0, has_side_effects=True, vmem_limit_bytes=32 * 1024 * 1024
         ),
     )(prior_disp, surface, springs, code)
 

time: 178 us -> 175 us (0.983)
  Pallas kernels: 168 us -> 164 us
    pallas_call x1, Pallas kernels: 168 us -> 164 us  [per_device(): pl.pallas_call(kernel, out_shape=(shape, shape), in_specs=[pl.BlockSpec(m...]
where the time goes in v3:
time: 175 us; the launch traced here: 173 us
  Pallas kernels  164 us (94%)
  local copies, waits for them, and re-layouts  7.39 us (4%)
    pallas_call x1, Pallas kernels, per_device(): pl.pallas_call(kernel, out_shape=(shape, shape), in_specs=[pl.BlockSpec(m...  164 us
    unnamed x6, local copies, waits for them, and re-layouts  6.62 us

profile of v3, /device:TPU:32, one launch (start us, length us, event | category | flops | bytes accessed | tf_op | source)
XLA Modules:
  0.0 172.7 jit_solution(8458392369416188292)
XLA Ops:
  0.6 0.7 compare_select_fusion
  1.4 0.8 reshape.10
  2.1 0.0 copy-start
  2.1 1.9 %copy-done = f32[2,3,2,128,512]{4,3,2,1,0:T(8,128)S(1)} copy-done((f32[2,3,2,128,512]{4,3,2,1,0:T(8,128)S(1)}, f32[2,3,2,128,512]{4,3,2,1,0:T(8,128)}, u32[]{:S(2)}) %copy-start) | copy-done | bytes 3145752
  4.0 0.0 copy-start.1
  4.0 1.4 copy-done.1
  5.4 163.9 %shard_map.68 = (f32[2,3,2,128,512]{4,3,2,1,0:T(8,128)S(1)}, f32[2,3,2,128,512]{4,3,2,1,0:T(8,128)S(1)}) custom-call(f32[2,3,2,128,512]{4,3,2,1,0:T(8,128)S(1)} %copy-done, f32[2,3,8,128]{3,2,1,0:T(8,128)S(1)} %copy.8.surface, f32[3,2,128,512]{3,2,1,0:T(8,128)S(1)} %copy-done.1, s32[8,128]{1,0:T(8,128)S(1)} %reshape.11.code), custom_call_target="tpu_custom_call" | custom-call | tf_op jit(solution)/shard_map/pallas_call | solution.py:378
  169.3 1.7 copy.11
  171.0 1.7 copy.12
  (2 shorter events, 0.0 us)
Async XLA Ops:
  2.1 1.9 %copy-start = (f32[2,3,2,128,512]{4,3,2,1,0:T(8,128)S(1)}, f32[2,3,2,128,512]{4,3,2,1,0:T(8,128)}, u32[]{:S(2)}) copy-start(f32[2,3,2,128,512]{4,3,2,1,0:T(8,128)} %prior.1) | copy-start | bytes 9437188
  4.0 1.4 copy-start.1

commit v4 on v3

--- a/solution.py
+++ b/solution.py
@@ -344,9 +344,9 @@
     start_out(0)
     begin_sweeps(2)
     sweeps(2, (1, 4), (2, 0))
-    start_vin(0)
     sweeps(2, (1, 6), (2, 2))
     start_out(1)
+    start_vin(0)
     sweeps(4, (2, 4))
     start_out(2)
     start_vin(1)

time: 175 us -> 170 us (0.971)
  Pallas kernels: 164 us -> 160 us
    pallas_call x1, Pallas kernels: 164 us -> 160 us  [per_device(): pl.pallas_call(kernel, out_shape=(shape, shape), in_specs=[pl.BlockSpec(m...]
where the time goes in v4:
time: 170 us; the launch traced here: 168 us
  Pallas kernels  160 us (94%)
  local copies, waits for them, and re-layouts  7.39 us (4%)
    pallas_call x1, Pallas kernels, per_device(): pl.pallas_call(kernel, out_shape=(shape, shape), in_specs=[pl.BlockSpec(m...  160 us
    unnamed x6, local copies, waits for them, and re-layouts  6.62 us

profile of v4, /device:TPU:32, one launch (start us, length us, event | category | flops | bytes accessed | tf_op | source)
XLA Modules:
  0.0 168.4 jit_solution(5309930090785287753)
XLA Ops:
  0.6 0.7 compare_select_fusion
  1.4 0.8 reshape.10
  2.1 0.0 copy-start
  2.1 1.9 %copy-done = f32[2,3,2,128,512]{4,3,2,1,0:T(8,128)S(1)} copy-done((f32[2,3,2,128,512]{4,3,2,1,0:T(8,128)S(1)}, f32[2,3,2,128,512]{4,3,2,1,0:T(8,128)}, u32[]{:S(2)}) %copy-start) | copy-done | bytes 3145752
  4.0 0.0 copy-start.1
  4.0 1.4 copy-done.1
  5.4 159.7 %shard_map.68 = (f32[2,3,2,128,512]{4,3,2,1,0:T(8,128)S(1)}, f32[2,3,2,128,512]{4,3,2,1,0:T(8,128)S(1)}) custom-call(f32[2,3,2,128,512]{4,3,2,1,0:T(8,128)S(1)} %copy-done, f32[2,3,8,128]{3,2,1,0:T(8,128)S(1)} %copy.8.surface, f32[3,2,128,512]{3,2,1,0:T(8,128)S(1)} %copy-done.1, s32[8,128]{1,0:T(8,128)S(1)} %reshape.11.code), custom_call_target="tpu_custom_call" | custom-call | tf_op jit(solution)/shard_map/pallas_call | solution.py:378
  165.1 1.7 copy.11
  166.7 1.7 copy.12
  (2 shorter events, 0.0 us)
Async XLA Ops:
  2.1 1.9 %copy-start = (f32[2,3,2,128,512]{4,3,2,1,0:T(8,128)S(1)}, f32[2,3,2,128,512]{4,3,2,1,0:T(8,128)}, u32[]{:S(2)}) copy-start(f32[2,3,2,128,512]{4,3,2,1,0:T(8,128)} %prior.1) | copy-start | bytes 9437188
  4.0 1.4 copy-start.1
